TPU v7x, 512 devices: a whole 4x8x8 slice. The times are simulated.
512 devices in a mesh: ct: 128 (over y, z, core), bl: 4 (over x).
Axes of the slice: x: 4, y: 8, z: 8, core: 2. Of those that a mesh axis runs over, the one named last changes fastest.
Arguments:
- samples: bfloat16 [1024, 65536], P('ct', 'bl'), may hold values from -6 to 6
- history: bfloat16 [1024, 1536], P('ct'), may hold values from -6 to 6
- tile_cell: int32 [256, 36], P('ct'), may hold values from 0 to 7
- tile_weight: float32 [256, 36], P('ct'), may hold values from 0.25 to 4
Outputs:
- grid: float32 [8, 256, 2, 128, 128], P('bl', 'ct')
All inputs are finite; a program needn't handle non-finite values.
Results may differ from a plain program's by a relative error of at most 0.0048.
Values may be sent and summed in bfloat16 or wider, within the bound.
A program may use at most 64 MiB of HBM per device.

v0:
```python
import math

import jax
import jax.numpy as jnp
from jax import lax
from jax.sharding import PartitionSpec as P

CH = 256
BLOCK = 128
TAPS = 4
SPECTRA = 128
CELL_DEV = 2
FRAME = 512


def from_behind(value, axis, by):
    size = lax.axis_size(axis)
    pairs = [(i, i + by) for i in range(size) if 0 <= i + by < size]
    return lax.ppermute(value, axis, pairs)


def filter_table():
    span = TAPS * FRAME
    sample_pos = jnp.arange(span, dtype=jnp.float32) + 0.5
    window = jnp.sinc(sample_pos / FRAME - TAPS / 2.0) * (
        0.5 - 0.5 * jnp.cos(2.0 * math.pi * sample_pos / span)
    )
    phase_int = (
        jnp.arange(FRAME, dtype=jnp.int32)[:, None]
        * jnp.arange(CH, dtype=jnp.int32)[None, :]
        % FRAME
    )
    angle = phase_int.astype(jnp.float32) * (2.0 * math.pi / FRAME)
    basis = jnp.concatenate([jnp.cos(angle), -jnp.sin(angle)], axis=1)
    table = window.reshape(TAPS, FRAME)[:, :, None] * basis[None] * (2.0 / math.sqrt(FRAME))
    return table.astype(jnp.bfloat16)


def cell_selector(tile_cell, weights, tri_index, is_valid, cell_count):
    picked = jnp.take(tile_cell, tri_index, axis=1)
    picked_weight = jnp.take(weights, tri_index, axis=1) * is_valid
    cell_ids = lax.broadcasted_iota(jnp.int32, (cell_count, 1, 1), 0)
    return (picked[None] == cell_ids).astype(jnp.float32) * picked_weight[None]


def shards(samples, history, tile_cell, tile_weight):
    bl_size = lax.axis_size("bl")
    bl_index = lax.axis_index("bl")
    inputs_dev = samples.shape[0]
    spec_dev = samples.shape[1] // FRAME
    table = filter_table()
    frames = samples.reshape(inputs_dev, spec_dev, FRAME)
    last_frames = frames[:, spec_dev - (TAPS - 1) :, :]
    earlier = from_behind(last_frames, "bl", 1)
    earlier = jnp.where(bl_index == 0, history.reshape(inputs_dev, TAPS - 1, FRAME), earlier)
    extended = jnp.concatenate([earlier, frames], axis=1)
    accum = jnp.zeros((2 * CH, inputs_dev, spec_dev), jnp.float32)
    for tap_index in range(TAPS):
        accum = accum + jnp.einsum(
            "psn,nk->kps",
            extended[:, tap_index : tap_index + spec_dev],
            table[tap_index],
            preferred_element_type=jnp.float32,
        )
    spectra = accum.astype(jnp.bfloat16).reshape(2, CH, inputs_dev, spec_dev)
    turned = lax.all_to_all(spectra, "ct", split_axis=1, concat_axis=2, tiled=True)
    channels = turned.shape[1]
    inputs = turned.shape[2]
    blocks = inputs // BLOCK
    cell_count = CELL_DEV * bl_size
    weights = tile_weight * (1.0 / math.sqrt(SPECTRA))
    rows_each = blocks // bl_size
    shard_part = lax.all_gather(turned, "bl", axis=3, tiled=True)
    row_part = lax.dynamic_slice_in_dim(
        shard_part, bl_index * rows_each * BLOCK, rows_each * BLOCK, 2
    )
    products = jnp.einsum(
        "acps,bcqs->cabpq", row_part, shard_part, preferred_element_type=jnp.float32
    )
    visibility = jnp.stack(
        [products[:, 0, 0] + products[:, 1, 1], products[:, 1, 0] - products[:, 0, 1]], axis=1
    )
    visibility = visibility.reshape(channels, 2, rows_each, BLOCK, blocks, BLOCK)
    row_index = bl_index * rows_each + jnp.arange(rows_each, dtype=jnp.int32)
    col_index = jnp.arange(blocks, dtype=jnp.int32)
    is_valid = col_index[None, :] >= row_index[:, None]
    tri_index = (
        row_index[:, None] * blocks
        - row_index[:, None] * (row_index[:, None] - 1) // 2
        + col_index[None, :]
        - row_index[:, None]
    )
    tri_index = jnp.where(is_valid, tri_index, 0).reshape(-1)
    selector = cell_selector(
        tile_cell, weights, tri_index, is_valid.reshape(-1).astype(jnp.float32), cell_count
    )
    selector = selector.reshape(cell_count, channels, rows_each, blocks)
    cell_term = jnp.einsum(
        "ecmj,cxmpjq->ecxpq", selector, visibility, precision=lax.Precision.HIGHEST
    )
    return lax.psum_scatter(cell_term, "bl", scatter_dimension=0, tiled=True)


def solution(mesh):
    return jax.shard_map(
        shards,
        mesh=mesh,
        in_specs=(P("ct", "bl"), P("ct", None), P("ct", None), P("ct", None)),
        out_specs=P("bl", "ct", None, None, None),
        check_vma=False,
    )
```

profile of v0, /device:TPU:1, one launch (start us, length us, event | category | flops | bytes accessed | tf_op | source)
XLA Modules:
  0.0 138.1 jit_solution(12725136759354073979)
XLA Ops:
  6.5 1.0 copy.82
  7.6 3.9 %collective-permute-start = (bf16[8,3,512]{2,1,0:T(4,128)(2,1)S(1)}, bf16[8,3,512]{2,1,0:T(4,128)(2,1)S(1)}, u32[]{:S(2)}, u32[]{:S(2)}) collective-permute-start(bf16[8,3,512]{2,1,0:T(4,128)(2,1)S(1)} %slice.53), channel_id=1, source_target_pairs={{0,1},{1,2},{2,3},{4,5},{5,6},{6,7},{8,9},{9,10},{10,11},{12,13},{... | collective-permute-start | bytes 73736 | tf_op jit(solution)/shard_map/ppermute | solution.py:19
  11.6 2.1 %sine_negate_fusion = (f32[512,256]{1,0:T(8,128)S(1)}, f32[512,256]{1,0:T(8,128)S(1)}) fusion(), kind=kLoop, calls=%fused_computation.30 | loop fusion | flops 1966080 | bytes 1048576 | tf_op jit(solution)/shard_map/neg | solution.py:34
  13.9 0.4 multiply_convert_fusion
  14.3 0.5 copy-done
  15.2 0.4 copy-done.1
  16.7 1.1 copy.52
  17.8 0.8 reshape.324
  18.6 32.0 %all_to_all.18 = bf16[128,2,512]{2,1,0:T(2,128)(2,1)S(1)} all-to-all(bf16[128,2,512]{2,1,0:T(2,128)(2,1)S(1)} %reshape.324), channel_id=1, replica_groups=mesh['ct'=128,'bl'=4] {'ct'}, dimensions={0} | all-to-all | bytes 524288 | tf_op jit(solution)/shard_map/all_to_all | solution.py:66
  50.6 0.5 reshape.325
  51.3 1.2 copy.55
  53.3 0.6 gather_fusion.1
  54.0 0.6 gather_fusion
  54.8 19.1 %all-gather.2.cloned.1.call-done = bf16[2,2,1024,128]{2,1,0,3:T(2,128)(2,1)} async-done(((bf16[2,2,1024,32]{2,1,0,3:T(2,128)(2,1)}), bf16[2,2,1024,128]{2,1,0,3:T(2,128)(2,1)}) %all-gather.2.cloned.1.call-update) | async-done | bytes 1048592 | tf_op jit(solution)/shard_map/all_gather | solution.py:73
  73.9 1.1 constant_dynamic-slice_fusion
  75.3 2.5 %convolution_bitcast_fusion = f32[2,2,2,256,1024]{3,4,1,2,0:T(8,128)S(1)} fusion(bf16[2,2,1024,128,1]{2,1,0,3,4:T(2,128)(2,1)} %bitcast.68, bf16[2,2,256,128]{3,2,0,1:T(8,128)(2,1)S(1)} %copy.74), kind=kOutput, calls=%fused_computation.7 | convolution fusion | flops 536870912 | bytes 9699328 | tf_op jit(solution)/shard_map/acps,bcqs->cabpq/dot_general | solution.py:77
  77.8 2.5 %slice_add_fusion = (f32[2,1,1,256,1024]{3,4,1,2,0:T(8,128)}, f32[2,1,1,256,1024]{3,4,1,2,0:T(8,128)}) fusion(f32[2,2,2,256,1024]{3,4,1,2,0:T(8,128)S(1)} %convolution_bitcast_fusion), kind=kLoop, calls=%fused_computation.9 | loop fusion | flops 1048576 | bytes 12582912 | tf_op jit(solution)/shard_map/add | solution.py:81
  80.3 2.3 %add.221 = f32[2,1,2,128,8,128]{3,2,5,4,0,1:T(2,128)S(1)} reshape(f32[2,1,1,256,1024]{3,4,1,2,0:T(8,128)} %get-tuple-element.5) | data formatting | bytes 4194304 | tf_op jit(solution)/shard_map/add | solution.py:81
  82.6 2.0 %copy.58 = f32[2,1,2,128,8,128]{5,4,2,3,1,0:T(8,128)} copy(f32[2,1,2,128,8,128]{3,2,5,4,0,1:T(2,128)S(1)} %add.221) | data formatting | bytes 4194304 | tf_op jit(solution)/shard_map/add | solution.py:81
  84.6 2.3 %sub.83 = f32[2,1,2,128,8,128]{3,2,5,4,0,1:T(2,128)S(1)} reshape(f32[2,1,1,256,1024]{3,4,1,2,0:T(8,128)} %get-tuple-element.6) | data formatting | bytes 4194304 | tf_op jit(solution)/shard_map/sub | solution.py:81
  86.9 2.0 %copy.59 = f32[2,1,2,128,8,128]{5,4,2,3,1,0:T(8,128)} copy(f32[2,1,2,128,8,128]{3,2,5,4,0,1:T(2,128)S(1)} %sub.83) | data formatting | bytes 4194304 | tf_op jit(solution)/shard_map/sub | solution.py:81
  89.0 4.0 %fusion.4 = f32[8,2,2,128,128]{4,0,3,2,1:T(8,128)S(1)} fusion(f32[2,1,2,128,8,128]{5,4,2,3,1,0:T(8,128)} %copy.59, f32[2,1,2,128,8,128]{5,4,2,3,1,0:T(8,128)} %copy.58, f32[2,2,8]{2,1,0:T(2,128)S(1)} %select_multiply_fusion, s32[2,2,8]{2,1,0:T(2,128)S(1)} %broadcast_select_fusion.1), kind=kOutput, calls=%fused_computation.10 | convolution fusion | flops 101712384 | bytes 6291712 | tf_op jit(solution)/shard_map/ecmj,cxmpjq->ecxpq/dot_general | solution.py:98
  93.0 1.7 %copy.64 = f32[8,2,2,128,128]{4,3,2,1,0:T(8,128)} copy(f32[8,2,2,128,128]{4,0,3,2,1:T(8,128)S(1)} %fusion.4) | data formatting | bytes 4194304 | tf_op jit(solution)/shard_map/ecmj,cxmpjq->ecxpq/transpose | solution.py:98
  94.7 36.5 %reduce-scatter.2.cloned.1.call-done = f32[2,2,2,128,128]{4,3,2,1,0:T(8,128)} async-done(((f32[8,2,2,128,128]{4,3,2,1,0:T(8,128)}), f32[2,2,2,128,128]{4,3,2,1,0:T(8,128)}) %reduce-scatter.2.cloned.1.call-update) | async-done | bytes 524304 | tf_op jit(solution)/shard_map/reduce_scatter | solution.py:101
  (40 shorter events, 3.2 us)
Async XLA Ops:
  6.5 67.4 %all-gather.2.cloned.1.call-start = ((), (), s32[]{:S(2)}) async-start(), calls=%async_computation.2 | async-start | bytes 1310720 | tf_op jit(solution)/shard_map/all_gather | solution.py:73
  7.6 8.0 %collective-permute-start = (bf16[8,3,512]{2,1,0:T(4,128)(2,1)S(1)}, bf16[8,3,512]{2,1,0:T(4,128)(2,1)S(1)}, u32[]{:S(2)}, u32[]{:S(2)}) collective-permute-start(bf16[8,3,512]{2,1,0:T(4,128)(2,1)S(1)} %slice.53), channel_id=1, source_target_pairs={{0,1},{1,2},{2,3},{4,5},{5,6},{6,7},{8,9},{9,10},{10,11},{12,13},{... | collective-permute-start | bytes 73736 | tf_op jit(solution)/shard_map/ppermute | solution.py:19
  13.9 1.0 copy-start
  14.8 0.7 copy-start.1
  51.1 2.1 %copy-start.2 = (f32[2,36]{1,0:T(2,128)S(1)}, f32[2,36]{1,0:T(2,128)}, u32[]{:S(2)}) copy-start(f32[2,36]{1,0:T(2,128)} %param.7) | copy-start | bytes 868
  51.1 2.8 %copy-start.3 = (s32[2,36]{1,0:T(2,128)S(1)}, s32[2,36]{1,0:T(2,128)}, u32[]{:S(2)}) copy-start(s32[2,36]{1,0:T(2,128)} %param.6) | copy-start | bytes 868
  52.5 78.7 %reduce-scatter.2.cloned.1.call-start = ((), (), s32[]{:S(2)}) async-start(), calls=%async_computation.3 | async-start | bytes 2621440 | tf_op jit(solution)/shard_map/reduce_scatter | solution.py:101
Sparse Core Ops, SparseCore 0:
  52.6 21.2 all-gather.1
  94.9 36.3 reduce-scatter.1
where the time goes:
time: 138 us
  waiting for transfers between devices  55.6 us (40%)
  blocking collectives  32 us (23%)
  local copies, waits for them, and re-layouts  19.5 us (14%)
  between operations  13.6 us (10%)
  matrix products  7.79 us (6%)
  other arithmetic  5.36 us (4%)
  starting transfers between devices  4.17 us (3%)
    reduce_scatter x1, waiting for transfers between devices, shards(): return lax.psum_scatter(cell_term, 'bl', scatter_dimension=0, tiled=True)  36.5 us
    all_to_all x1, blocking collectives, shards(): lax.all_to_all(spectra, 'ct', split_axis=1, concat_axis=2, tiled=True)  32 us
    all_gather x1, waiting for transfers between devices, shards(): shard_part = lax.all_gather(turned, 'bl', axis=3, tiled=True)  19.1 us
    sub x2, local copies, waits for them, and re-layouts, shards(): products[:, 1, 0] - products[:, 0, 1]  4.33 us
    add x2, local copies, waits for them, and re-layouts, shards(): products[:, 0, 0] + products[:, 1, 1]  4.33 us
    dot_general x1, matrix products, shards(): jnp.einsum('ecmj,cxmpjq->ecxpq', selector, visibility, precision=lax.Prec...  4.02 us
    ppermute x1, starting transfers between devices, from_behind(): return lax.ppermute(value, axis, pairs)  3.95 us
    unnamed x13, local copies, waits for them, and re-layouts  3.65 us
  transfers between devices with their start and end apart: 3, of which 2 were waited for; matrix products, arithmetic and copies ran while one was open for 4% of the time, Pallas kernels for 0%

commit v1 on v0

v1 whole, which is shorter than its diff:
```python
import functools
import math

import jax
import jax.numpy as jnp
import numpy as np
from jax import lax
from jax.experimental import pallas as pl
from jax.experimental.pallas import tpu as pltpu
from jax.sharding import PartitionSpec as P

MESH = pl.DeviceIdType.MESH
BF16 = jnp.bfloat16
F32 = jnp.float32

CH = 256
BLOCK = 128
TAPS = 4
SPECTRA = 128
FRAME = 512
NTILE = 36
CELL_DEV = 2
RING = 8
NX = 4
ROWS = 8
SPEC_DEV = SPECTRA // NX
HALO = TAPS - 1
OFFSETS = (4, 3, 5, 2, 6, 1, 7)


def filter_table():
    span = TAPS * FRAME
    pos = np.arange(span, dtype=np.float32) + np.float32(0.5)
    window = np.sinc(pos / np.float32(FRAME) - np.float32(TAPS / 2.0)).astype(np.float32) * (
        np.float32(0.5) - np.float32(0.5) * np.cos(np.float32(2.0 * math.pi) * pos / np.float32(span))
    )
    phase = np.arange(FRAME)[:, None] * np.arange(CH)[None, :] % FRAME
    angle = phase.astype(np.float32) * np.float32(2.0 * math.pi / FRAME)
    basis = np.concatenate([np.cos(angle), -np.sin(angle)], axis=1).astype(np.float32)
    table = window.astype(np.float32).reshape(TAPS, FRAME)[:, :, None] * basis[None]
    table = table * np.float32(2.0 / math.sqrt(FRAME))
    part, core, chip = np.meshgrid(np.arange(4), np.arange(2), np.arange(64), indexing="ij")
    column = (part % 2) * CH + 2 * (2 * chip + core) + part // 2
    return np.ascontiguousarray(table[:, :, column.reshape(-1)].transpose(0, 2, 1)).astype(BF16)


def swap_step(pair, bit, lane):
    low, high = pair
    clear = (lane & bit) == 0
    return (
        jnp.where(clear, low, pltpu.roll(high, bit, 1)),
        jnp.where(clear, pltpu.roll(low, 128 - bit, 1), high),
    )


def kernel(
    samples, history, table, cells, weights, out,
    tab, smp, halo, even, odd, spec, turn, hold, mid, full, rhs, lhs, wsm,
    tab_sem, smp_sem, halo_send, halo_recv, core_sem, own_sem, p1_send, p1_recv, p2_send, p2_recv, ag_send, ag_recv,
):
    ct = lax.axis_index("ct")
    bl = lax.axis_index("bl")
    y = ct // 16
    z = lax.rem(ct // 2, RING)
    c = lax.rem(ct, 2)

    def on(yy, zz, cc):
        return (yy * 16 + zz * 2 + cc, bl)

    barrier = pltpu.get_barrier_semaphore()

    def greet(device):
        pl.semaphore_signal(barrier, inc=1, device_id=device, device_id_type=MESH)

    for k in range(1, NX):
        greet((ct, lax.rem(bl + k, NX)))
    greet(on(y, z, 1 - c))
    for k in range(1, RING):
        greet(on(lax.rem(y + k, RING), z, c))
        greet(on(y, lax.rem(z + k, RING), c))

    smp_copy = pltpu.make_async_copy(samples, smp, smp_sem)
    smp_copy.start()
    tab_copies = []
    for t in range(TAPS):
        tab_copies.append(pltpu.make_async_copy(table.at[t], tab.at[t], tab_sem.at[t]))
        tab_copies[-1].start()

    def one_weight(t, carry):
        for ch in range(2):
            scaled = weights[ch, t] * (1.0 / math.sqrt(SPECTRA))
            for e in range(CELL_DEV):
                wsm[ch, e, t] = jnp.where(cells[ch, t] == bl * CELL_DEV + e, scaled, 0.0)
        return carry

    lax.fori_loop(0, NTILE, one_weight, 0)

    pl.semaphore_wait(barrier, NX - 1 + 1 + 2 * (RING - 1))

    halo_copy = pltpu.make_async_remote_copy(
        src_ref=samples.at[:, pl.ds((SPEC_DEV - HALO) * FRAME, HALO * FRAME)],
        dst_ref=halo,
        send_sem=halo_send,
        recv_sem=halo_recv,
        device_id=(ct, lax.rem(bl + 1, NX)),
        device_id_type=MESH,
    )
    hist_copy = pltpu.make_async_copy(history, halo, own_sem.at[2])

    @pl.when(bl < NX - 1)
    def _():
        halo_copy.start()

    @pl.when(bl == 0)
    def _():
        hist_copy.start()

    def put(ext, value):
        even[pl.ds(8 * ext, 8), :] = value
        if ext >= 1:
            odd[pl.ds(8 * (ext - 1), 8), :] = value

    smp_copy.wait()
    for f in range(SPEC_DEV):
        put(f + HALO, smp[:, pl.ds(f * FRAME, FRAME)])

    @pl.when(bl < NX - 1)
    def _():
        halo_copy.wait_send()

    @pl.when(bl == 0)
    def _():
        hist_copy.wait()

    @pl.when(bl > 0)
    def _():
        halo_copy.wait_recv()

    for f in range(HALO):
        put(f, halo[:, pl.ds(f * FRAME, FRAME)])

    total = None
    for t in range(TAPS):
        tab_copies[t].wait()
        source = (even, odd)[t % 2]
        term = lax.dot_general(
            tab[t], source[pl.ds(16 * (t // 2), 256), :], (((1,), (1,)), ((), ())), preferred_element_type=F32
        )
        total = term if total is None else total + term
    spec[...] = total

    lane = lax.broadcasted_iota(jnp.int32, (8, 128), 1)
    for g in range(16):
        v = [spec[pl.ds(q * 128 + g * 8, 8), pl.ds(h * 128, 128)] for q in range(4) for h in range(2)]
        for bit in (1, 2, 4):
            for i in range(8):
                if not i & bit:
                    v[i], v[i | bit] = swap_step((v[i], v[i | bit]), bit, lane)
        for p in range(ROWS):
            turn[pl.ds(g * 64 + p, 8, stride=8), :] = v[p]
        core = g // 8
        other = lax.rem(c + core, 2)
        slot = core * (1 - other) + 2 * other
        chips = g % 8
        hold[slot, chips] = turn[pl.ds(g * 64, 64), :].astype(BF16).reshape(8, 8, 128)

    swap = pltpu.make_async_remote_copy(
        src_ref=hold.at[2], dst_ref=hold.at[c], send_sem=core_sem.at[0], recv_sem=core_sem.at[1],
        device_id=on(y, z, 1 - c), device_id_type=MESH,
    )
    swap.start()
    swap.wait_recv()

    def turn_corner(first_is_z):
        me1, me2 = (z, y) if first_is_z else (y, z)

        def there(phase, k):
            if (phase == 1) == first_is_z:
                return on(y, lax.rem(z + k, RING), c)
            return on(lax.rem(y + k, RING), z, c)

        def part(ref, i, by_z):
            return ref.at[:, :, i] if by_z else ref.at[:, i]

        both = hold.at[pl.ds(0, 2)]
        mine = full.at[bl]
        first = []
        for n, k in enumerate(OFFSETS):
            first.append(pltpu.make_async_remote_copy(
                src_ref=part(both, lax.rem(me1 + k, RING), first_is_z), dst_ref=part(mid, me1, first_is_z),
                send_sem=p1_send.at[n], recv_sem=p1_recv.at[n], device_id=there(1, k), device_id_type=MESH,
            ))
            first[-1].start()
        keep = pltpu.make_async_copy(part(both, me1, first_is_z), part(mid, me1, first_is_z), own_sem.at[0])
        keep.start()
        for copy in first:
            copy.wait_recv()
        keep.wait()
        second = []
        for n, k in enumerate(OFFSETS):
            second.append(pltpu.make_async_remote_copy(
                src_ref=part(mid, lax.rem(me2 + k, RING), not first_is_z), dst_ref=part(mine, me2, not first_is_z),
                send_sem=p2_send.at[n], recv_sem=p2_recv.at[n], device_id=there(2, k), device_id_type=MESH,
            ))
            second[-1].start()
        keep = pltpu.make_async_copy(part(mid, me2, not first_is_z), part(mine, me2, not first_is_z), own_sem.at[1])
        keep.start()
        spread = []
        for n, k in enumerate((0,) + OFFSETS):
            if n == 0:
                keep.wait()
            else:
                second[n - 1].wait_recv()
            chunk = part(mine, lax.rem(me2 + RING - k, RING), not first_is_z)
            for o in (2, 1, 3):
                spread.append(pltpu.make_async_remote_copy(
                    src_ref=chunk, dst_ref=chunk, send_sem=ag_send.at[o - 1, n], recv_sem=ag_recv.at[o - 1, n],
                    device_id=(ct, lax.rem(bl + o, NX)), device_id_type=MESH,
                ))
                spread[-1].start()
        for copy in spread:
            copy.wait_recv()
        for copy in first + second + spread:
            copy.wait_send()

    @pl.when(c == 0)
    def _():
        turn_corner(True)

    @pl.when(c == 1)
    def _():
        turn_corner(False)

    swap.wait_send()

    lane = lax.broadcasted_iota(jnp.int32, (16, 128), 1)
    real = (lane & 2) == 0

    def operands(n, carry):
        j, zz = n // RING, lax.rem(n, RING)
        rows = pl.ds(pl.multiple_of(zz * 16, 16), 16)
        under = pl.ds(pl.multiple_of(128 + zz * 16, 16), 16)
        d = [full[b, :, j, zz].astype(F32).reshape(16, 128) for b in range(NX)]
        for half in range(2):
            pair = swap_step((d[2 * half], d[2 * half + 1]), 4, lane)
            for ch in range(2):
                x = pair[ch]
                r = jnp.where(real, -pltpu.roll(x, 126, 1), pltpu.roll(x, 2, 1))
                cols = pl.ds(pl.multiple_of(j * 256 + half * 128, 128), 128)
                rhs[ch, rows, cols] = x.astype(BF16)
                rhs[ch, under, cols] = r.astype(BF16)
        return carry

    lax.fori_loop(0, RING * RING, operands, 0)

    def fold(zz, carry):
        rows = pl.ds(pl.multiple_of(zz * 16, 16), 16)
        for ch in range(2):
            x = [rhs[ch, rows, i * 256:(i + 1) * 256].astype(F32) for i in range(8)]
            for e in range(CELL_DEV):
                place = pl.ds(pl.multiple_of(e * 128 + zz * 16, 16), 16)
                for j in range(8):
                    acc = None
                    for i in range(j + 1):
                        t = i * 8 - i * (i - 1) // 2 + j - i
                        term = x[i] * wsm[ch, e, t]
                        acc = term if acc is None else acc + term
                    lhs[ch, place, j * 256:(j + 1) * 256] = acc.astype(BF16)
        return carry

    lax.fori_loop(0, RING, fold, 0)

    for ch in range(2):
        result = lax.dot_general(lhs[ch], rhs[ch], (((1,), (1,)), ((), ())), preferred_element_type=F32)
        for e in range(CELL_DEV):
            for x in range(2):
                out[e, ch, x] = result[e * 128:(e + 1) * 128, x * 128:(x + 1) * 128]


def shards(samples, history, tile_cell, tile_weight):
    table = jnp.asarray(filter_table())
    any_space = pl.BlockSpec(memory_space=pl.ANY)
    smem = pl.BlockSpec(memory_space=pltpu.SMEM)
    dma = pltpu.SemaphoreType.DMA
    return pl.pallas_call(
        kernel,
        out_shape=jax.ShapeDtypeStruct((CELL_DEV, 2, 2, BLOCK, BLOCK), F32),
        in_specs=[any_space, any_space, any_space, smem, smem],
        out_specs=pl.BlockSpec(memory_space=pltpu.VMEM),
        scratch_shapes=[
            pltpu.VMEM((TAPS, 2 * CH, FRAME), BF16),
            pltpu.VMEM((8, SPEC_DEV * FRAME), BF16),
            pltpu.VMEM((8, HALO * FRAME), BF16),
            pltpu.VMEM((288, FRAME), BF16),
            pltpu.VMEM((288, FRAME), BF16),
            pltpu.VMEM((512, 256), F32),
            pltpu.VMEM((1024, 128), F32),
            pltpu.VMEM((3, RING, RING, 8, 128), BF16),
            pltpu.VMEM((2, RING, RING, 8, 128), BF16),
            pltpu.VMEM((NX, 2, RING, RING, 8, 128), BF16),
            pltpu.VMEM((2, 256, 2048), BF16),
            pltpu.VMEM((2, 256, 2048), BF16),
            pltpu.SMEM((2, CELL_DEV, NTILE), F32),
            dma((TAPS,)),
            dma,
            dma,
            dma,
            dma((2,)),
            dma((3,)),
            dma((RING - 1,)),
            dma((RING - 1,)),
            dma((RING - 1,)),
            dma((RING - 1,)),
            dma((NX - 1, RING)),
            dma((NX - 1, RING)),
        ],
        compiler_params=pltpu.CompilerParams(
            collective_id=0, has_side_effects=True, vmem_limit_bytes=60 * 1024 * 1024
        ),
    )(samples, history, table, tile_cell, tile_weight)


def solution(mesh):
    return jax.shard_map(
        shards,
        mesh=mesh,
        in_specs=(P("ct", "bl"), P("ct", None), P("ct", None), P("ct", None)),
        out_specs=P("bl", "ct", None, None, None),
        check_vma=False,
    )
```

time: 138 us -> 59.7 us (0.43)
  Pallas kernels: 0 us -> 57.6 us
  waiting for transfers between devices: 55.6 us -> 0 us
  blocking collectives: 32 us -> 0 us
  local copies, waits for them, and re-layouts: 19.5 us -> 1.87 us
  between operations: 13.6 us -> 0.01 us
  matrix products: 7.79 us -> 0 us
  other arithmetic: 5.36 us -> 0 us
  starting transfers between devices: 4.17 us -> 0 us
    pallas_call x0 -> x1, Pallas kernels: none -> 57.6 us  [shards(): pl.pallas_call(kernel, out_shape=jax.ShapeDtypeStruct((CELL_DEV, 2, 2, BL...]
    reduce_scatter x1 -> x0, waiting for transfers between devices: 36.5 us -> none  [shards(): return lax.psum_scatter(cell_term, 'bl', scatter_dimension=0, tiled=True)]
    all_to_all x1 -> x0, blocking collectives: 32 us -> none  [shards(): lax.all_to_all(spectra, 'ct', split_axis=1, concat_axis=2, tiled=True)]
    all_gather x1 -> x0, waiting for transfers between devices: 19.1 us -> none  [shards(): shard_part = lax.all_gather(turned, 'bl', axis=3, tiled=True)]
    dot_general x6 -> x0, matrix products: 7.79 us -> none  [the longest x1 4.02 us: shards(): jnp.einsum('ecmj,cxmpjq->ecxpq', selector, visibility, precision=lax.Prec...]
    add x4 -> x0, local copies, waits for them, and re-layouts: 4.48 us -> none  [the longest x2 4.33 us: shards(): products[:, 0, 0] + products[:, 1, 1]]
    sub x2 -> x0, local copies, waits for them, and re-layouts: 4.33 us -> none  [shards(): products[:, 1, 0] - products[:, 0, 1]]
    ppermute x1 -> x0, starting transfers between devices: 3.95 us -> none  [from_behind(): return lax.ppermute(value, axis, pairs)]
  transfers between devices with their start and end apart: 3 -> 0, of which waited for: 2 -> 0; matrix products, arithmetic and copies ran while one was open for 4% -> 0% of each run, Pallas kernels for 0% -> 0%
where the time goes in v1:
time: 59.7 us; the launch traced here: 59.5 us
  Pallas kernels  57.6 us (96%)
  local copies, waits for them, and re-layouts  1.87 us (3%)
    pallas_call x1, Pallas kernels, shards(): pl.pallas_call(kernel, out_shape=jax.ShapeDtypeStruct((CELL_DEV, 2, 2, BL...  57.6 us
    unnamed x1, local copies, waits for them, and re-layouts  1.87 us

profile of v1, /device:TPU:1, one launch (start us, length us, event | category | flops | bytes accessed | tf_op | source)
XLA Modules:
  0.0 59.5 jit_solution(3967252524476926907)
XLA Ops:
  0.0 57.6 %shard_map.55 = f32[2,2,2,128,128]{4,3,2,1,0:T(8,128)} custom-call(bf16[8,16384]{1,0:T(8,128)(2,1)} %samples.1, bf16[8,1536]{1,0:T(8,128)(2,1)} %history.1, bf16[4,512,512]{2,1,0:T(8,128)(2,1)} %constant.2.clone.table, s32[2,36]{1,0:T(2,128)} %cells.1, f32[2,36]{1,0:T(2,128)} %weights.1), custom_call_target="tpu_custom_call" | custom-call | tf_op jit(solution)/shard_map/pallas_call | solution.py:285
  57.6 1.9 %copy.7 = f32[2,2,2,128,128]{4,3,2,1,0:T(8,128)} copy(f32[2,2,2,128,128]{4,3,2,1,0:T(8,128)} %shard_map.55) | data formatting | bytes 1048576

commit v2 on v1

--- a/solution.py
+++ b/solution.py
@@ -25,6 +25,7 @@
 ROWS = 8
 SPEC_DEV = SPECTRA // NX
 HALO = TAPS - 1
+UNROLL = 8
 OFFSETS = (4, 3, 5, 2, 6, 1, 7)
 
 
@@ -54,9 +55,9 @@
 
 
 def kernel(
-    samples, history, table, cells, weights, out,
-    tab, smp, halo, even, odd, spec, turn, hold, mid, full, rhs, lhs, wsm,
-    tab_sem, smp_sem, halo_send, halo_recv, core_sem, own_sem, p1_send, p1_recv, p2_send, p2_recv, ag_send, ag_recv,
+    samples, history, table, cells_hbm, weights_hbm, out,
+    tab, smp, halo, even, odd, spec, turn, hold, mid, full, rhs, lhs, wsm, cells, weights,
+    tab_sem, smp_sem, cell_sem, halo_send, halo_recv, core_sem, own_sem, p1_send, p1_recv, p2_send, p2_recv, ag_send, ag_recv,
 ):
     ct = lax.axis_index("ct")
     bl = lax.axis_index("bl")
@@ -81,19 +82,16 @@
 
     smp_copy = pltpu.make_async_copy(samples, smp, smp_sem)
     smp_copy.start()
+    cell_copies = [
+        pltpu.make_async_copy(cells_hbm, cells, cell_sem.at[0]),
+        pltpu.make_async_copy(weights_hbm, weights, cell_sem.at[1]),
+    ]
+    for copy in cell_copies:
+        copy.start()
     tab_copies = []
     for t in range(TAPS):
         tab_copies.append(pltpu.make_async_copy(table.at[t], tab.at[t], tab_sem.at[t]))
         tab_copies[-1].start()
-
-    def one_weight(t, carry):
-        for ch in range(2):
-            scaled = weights[ch, t] * (1.0 / math.sqrt(SPECTRA))
-            for e in range(CELL_DEV):
-                wsm[ch, e, t] = jnp.where(cells[ch, t] == bl * CELL_DEV + e, scaled, 0.0)
-        return carry
-
-    lax.fori_loop(0, NTILE, one_weight, 0)
 
     pl.semaphore_wait(barrier, NX - 1 + 1 + 2 * (RING - 1))
 
@@ -105,7 +103,7 @@
         device_id=(ct, lax.rem(bl + 1, NX)),
         device_id_type=MESH,
     )
-    hist_copy = pltpu.make_async_copy(history, halo, own_sem.at[2])
+    hist_copy = pltpu.make_async_copy(history, halo, own_sem.at[4])
 
     @pl.when(bl < NX - 1)
     def _():
@@ -169,89 +167,140 @@
         device_id=on(y, z, 1 - c), device_id_type=MESH,
     )
     swap.start()
-    swap.wait_recv()
-
-    def turn_corner(first_is_z):
-        me1, me2 = (z, y) if first_is_z else (y, z)
-
-        def there(phase, k):
-            if (phase == 1) == first_is_z:
-                return on(y, lax.rem(z + k, RING), c)
-            return on(lax.rem(y + k, RING), z, c)
-
-        def part(ref, i, by_z):
-            return ref.at[:, :, i] if by_z else ref.at[:, i]
-
-        both = hold.at[pl.ds(0, 2)]
-        mine = full.at[bl]
-        first = []
-        for n, k in enumerate(OFFSETS):
-            first.append(pltpu.make_async_remote_copy(
-                src_ref=part(both, lax.rem(me1 + k, RING), first_is_z), dst_ref=part(mid, me1, first_is_z),
-                send_sem=p1_send.at[n], recv_sem=p1_recv.at[n], device_id=there(1, k), device_id_type=MESH,
-            ))
-            first[-1].start()
-        keep = pltpu.make_async_copy(part(both, me1, first_is_z), part(mid, me1, first_is_z), own_sem.at[0])
-        keep.start()
-        for copy in first:
-            copy.wait_recv()
-        keep.wait()
-        second = []
-        for n, k in enumerate(OFFSETS):
-            second.append(pltpu.make_async_remote_copy(
-                src_ref=part(mid, lax.rem(me2 + k, RING), not first_is_z), dst_ref=part(mine, me2, not first_is_z),
-                send_sem=p2_send.at[n], recv_sem=p2_recv.at[n], device_id=there(2, k), device_id_type=MESH,
-            ))
-            second[-1].start()
-        keep = pltpu.make_async_copy(part(mid, me2, not first_is_z), part(mine, me2, not first_is_z), own_sem.at[1])
-        keep.start()
-        spread = []
-        for n, k in enumerate((0,) + OFFSETS):
-            if n == 0:
-                keep.wait()
-            else:
-                second[n - 1].wait_recv()
-            chunk = part(mine, lax.rem(me2 + RING - k, RING), not first_is_z)
-            for o in (2, 1, 3):
-                spread.append(pltpu.make_async_remote_copy(
-                    src_ref=chunk, dst_ref=chunk, send_sem=ag_send.at[o - 1, n], recv_sem=ag_recv.at[o - 1, n],
-                    device_id=(ct, lax.rem(bl + o, NX)), device_id_type=MESH,
-                ))
-                spread[-1].start()
-        for copy in spread:
-            copy.wait_recv()
-        for copy in first + second + spread:
-            copy.wait_send()
-
-    @pl.when(c == 0)
-    def _():
-        turn_corner(True)
-
-    @pl.when(c == 1)
-    def _():
-        turn_corner(False)
-
-    swap.wait_send()
-
-    lane = lax.broadcasted_iota(jnp.int32, (16, 128), 1)
-    real = (lane & 2) == 0
-
-    def operands(n, carry):
-        j, zz = n // RING, lax.rem(n, RING)
+
+    for copy in cell_copies:
+        copy.wait()
+
+    def one_weight(t, carry):
+        for ch in range(2):
+            scaled = weights[ch, t] * (1.0 / math.sqrt(SPECTRA))
+            for e in range(CELL_DEV):
+                wsm[ch, e, t] = jnp.where(cells[ch, t] == bl * CELL_DEV + e, scaled, 0.0)
+        return carry
+
+    lax.fori_loop(0, NTILE, one_weight, 0)
+
+    lane16 = lax.broadcasted_iota(jnp.int32, (16, 128), 1)
+    real = (lane16 & 2) == 0
+
+    def operands(j, zz):
         rows = pl.ds(pl.multiple_of(zz * 16, 16), 16)
         under = pl.ds(pl.multiple_of(128 + zz * 16, 16), 16)
         d = [full[b, :, j, zz].astype(F32).reshape(16, 128) for b in range(NX)]
         for half in range(2):
-            pair = swap_step((d[2 * half], d[2 * half + 1]), 4, lane)
+            pair = swap_step((d[2 * half], d[2 * half + 1]), 4, lane16)
             for ch in range(2):
                 x = pair[ch]
                 r = jnp.where(real, -pltpu.roll(x, 126, 1), pltpu.roll(x, 2, 1))
                 cols = pl.ds(pl.multiple_of(j * 256 + half * 128, 128), 128)
                 rhs[ch, rows, cols] = x.astype(BF16)
                 rhs[ch, under, cols] = r.astype(BF16)
-        return carry
-
-    lax.fori_loop(0, RING * RING, operands, 0)
+
+    def turn_corner(mine_core):
+        first_is_z = mine_core == 0
+        me1, me2 = (z, y) if first_is_z else (y, z)
+
+        def there(phase, k):
+            if (phase == 1) == first_is_z:
+                return on(y, lax.rem(z + k, RING), c)
+            return on(lax.rem(y + k, RING), z, c)
+
+        def part(ref, i, phase):
+            return ref.at[:, i] if (phase == 1) == first_is_z else ref.at[i]
+
+        first, keep1, second, keep2, spread = [], [], [], [], {}
+
+        def start_first(h):
+            source, target = hold.at[(mine_core + h) % 2], mid.at[(mine_core + h) % 2]
+            copies = [
+                pltpu.make_async_remote_copy(
+                    src_ref=part(source, lax.rem(me1 + k, RING), 1), dst_ref=part(target, me1, 1),
+                    send_sem=p1_send.at[h, n], recv_sem=p1_recv.at[h, n], device_id=there(1, k), device_id_type=MESH,
+                )
+                for n, k in enumerate(OFFSETS)
+            ]
+            for copy in copies:
+                copy.start()
+            keep = pltpu.make_async_copy(part(source, me1, 1), part(target, me1, 1), own_sem.at[h])
+            keep.start()
+            first.append(copies)
+            keep1.append(keep)
+
+        def share(h, n, k, source):
+            target = part(full.at[bl, (mine_core + h) % 2], lax.rem(me2 + RING - k, RING), 2)
+            copies = [
+                pltpu.make_async_remote_copy(
+                    src_ref=target if source is None else source, dst_ref=target,
+                    send_sem=ag_send.at[o - 1, h, n], recv_sem=ag_recv.at[o - 1, h, n],
+                    device_id=(ct, lax.rem(bl + o, NX)), device_id_type=MESH,
+                )
+                for o in (2, 1, 3)
+            ]
+            for copy in copies:
+                copy.start()
+            spread[h, n] = copies
+
+        def start_second(h):
+            source, target = mid.at[(mine_core + h) % 2], full.at[bl, (mine_core + h) % 2]
+            for copy in first[h]:
+                copy.wait_recv()
+            keep1[h].wait()
+            copies = [
+                pltpu.make_async_remote_copy(
+                    src_ref=part(source, lax.rem(me2 + k, RING), 2), dst_ref=part(target, me2, 2),
+                    send_sem=p2_send.at[h, n], recv_sem=p2_recv.at[h, n], device_id=there(2, k), device_id_type=MESH,
+                )
+                for n, k in enumerate(OFFSETS)
+            ]
+            for copy in copies:
+                copy.start()
+            share(h, 0, 0, part(source, me2, 2))
+            keep = pltpu.make_async_copy(part(source, me2, 2), part(target, me2, 2), own_sem.at[2 + h])
+            keep.start()
+            second.append(copies)
+            keep2.append(keep)
+
+        start_first(0)
+        swap.wait_recv()
+        start_first(1)
+        start_second(0)
+        start_second(1)
+        for h in range(2):
+            for n, k in enumerate(OFFSETS):
+                second[h][n].wait_recv()
+                share(h, n + 1, k, None)
+        keep2[0].wait()
+        keep2[1].wait()
+        for n, k in enumerate((0,) + OFFSETS):
+            for h in range(2):
+                for copy in spread[h, n]:
+                    copy.wait_recv()
+            chunk = lax.rem(me2 + RING - k, RING)
+
+            def one(i, carry):
+                if first_is_z:
+                    operands(chunk, i)
+                else:
+                    operands(i, chunk)
+                return carry
+
+            lax.fori_loop(0, RING, one, 0, unroll=UNROLL)
+        for h in range(2):
+            for copy in first[h] + second[h]:
+                copy.wait_send()
+            for n in range(RING):
+                for copy in spread[h, n]:
+                    copy.wait_send()
+
+    @pl.when(c == 0)
+    def _():
+        turn_corner(0)
+
+    @pl.when(c == 1)
+    def _():
+        turn_corner(1)
+
+    swap.wait_send()
 
     def fold(zz, carry):
         rows = pl.ds(pl.multiple_of(zz * 16, 16), 16)
@@ -279,13 +328,12 @@
 
 def shards(samples, history, tile_cell, tile_weight):
     table = jnp.asarray(filter_table())
-    any_space = pl.BlockSpec(memory_space=pl.ANY)
-    smem = pl.BlockSpec(memory_space=pltpu.SMEM)
+    hbm = pl.BlockSpec(memory_space=pltpu.HBM)
     dma = pltpu.SemaphoreType.DMA
     return pl.pallas_call(
         kernel,
         out_shape=jax.ShapeDtypeStruct((CELL_DEV, 2, 2, BLOCK, BLOCK), F32),
-        in_specs=[any_space, any_space, any_space, smem, smem],
+        in_specs=[hbm] * 5,
         out_specs=pl.BlockSpec(memory_space=pltpu.VMEM),
         scratch_shapes=[
             pltpu.VMEM((TAPS, 2 * CH, FRAME), BF16),
@@ -301,23 +349,26 @@
             pltpu.VMEM((2, 256, 2048), BF16),
             pltpu.VMEM((2, 256, 2048), BF16),
             pltpu.SMEM((2, CELL_DEV, NTILE), F32),
+            pltpu.SMEM((2, NTILE), jnp.int32),
+            pltpu.SMEM((2, NTILE), F32),
             dma((TAPS,)),
             dma,
+            dma((2,)),
             dma,
             dma,
             dma((2,)),
-            dma((3,)),
-            dma((RING - 1,)),
-            dma((RING - 1,)),
-            dma((RING - 1,)),
-            dma((RING - 1,)),
-            dma((NX - 1, RING)),
-            dma((NX - 1, RING)),
+            dma((5,)),
+            dma((2, RING - 1)),
+            dma((2, RING - 1)),
+            dma((2, RING - 1)),
+            dma((2, RING - 1)),
+            dma((NX - 1, 2, RING)),
+            dma((NX - 1, 2, RING)),
         ],
         compiler_params=pltpu.CompilerParams(
-            collective_id=0, has_side_effects=True, vmem_limit_bytes=60 * 1024 * 1024
+            collective_id=0, has_side_effects=True, vmem_limit_bytes=40 * 1024 * 1024
         ),
-    )(samples, history, table, tile_cell, tile_weight)
+    )(*[pltpu.with_memory_space_constraint(v, pltpu.HBM) for v in (samples, history, table, tile_cell, tile_weight)])
 
 
 def solution(mesh):

time: 59.7 us -> 44 us (0.74)
  the two profiles are of different devices: /device:TPU:1 before, /device:TPU:8 now
where the time goes in v2:
time: 44 us; the launch traced here: 43.9 us
  Pallas kernels  43.1 us (98%)
  local copies, waits for them, and re-layouts  0.8 us (2%)
    pallas_call x1, Pallas kernels, shards(): pl.pallas_call(kernel, out_shape=jax.ShapeDtypeStruct((CELL_DEV, 2, 2, BL...  43.1 us

profile of v2, /device:TPU:8, one launch (start us, length us, event | category | flops | bytes accessed | tf_op | source)
XLA Modules:
  0.0 43.9 jit_solution(12577610167533639857)
XLA Ops:
  0.0 43.1 %shard_map.55 = f32[2,2,2,128,128]{4,3,2,1,0:T(8,128)S(1)} custom-call(bf16[8,16384]{1,0:T(8,128)(2,1)} %samples.1, bf16[8,1536]{1,0:T(8,128)(2,1)} %history.1, bf16[4,512,512]{2,1,0:T(8,128)(2,1)} %constant.2.clone.table, s32[2,36]{1,0:T(2,128)} %cells_hbm.1, f32[2,36]{1,0:T(2,128)} %weights_hbm.1), custom_call_target="tpu_custom_call" | custom-call | tf_op jit(solution)/shard_map/pallas_call | solution.py:333
  43.1 0.8 %copy.7 = f32[2,2,2,128,128]{4,3,2,1,0:T(8,128)} copy(f32[2,2,2,128,128]{4,3,2,1,0:T(8,128)S(1)} %shard_map.55) | data formatting | bytes 1048576

commit v3 on v2

v3 whole, which is shorter than its diff:
```python
import functools
import math

import jax
import jax.numpy as jnp
import numpy as np
from jax import lax
from jax.experimental import pallas as pl
from jax.experimental.pallas import tpu as pltpu
from jax.sharding import PartitionSpec as P

MESH = pl.DeviceIdType.MESH
BF16 = jnp.bfloat16
F32 = jnp.float32

CH = 256
BLOCK = 128
TAPS = 4
SPECTRA = 128
FRAME = 512
NTILE = 36
CELL_DEV = 2
RING = 8
NX = 4
ROWS = 8
SPEC_DEV = SPECTRA // NX
HALO = TAPS - 1


def offset(n):
    m = n - 1
    odd = m % 2
    return (1 - (n == 0)) * (4 + (1 - odd) * (m // 2) - odd * ((m + 1) // 2))


OFFSETS = tuple(offset(n) for n in range(1, RING))


def filter_table():
    span = TAPS * FRAME
    pos = np.arange(span, dtype=np.float32) + np.float32(0.5)
    window = np.sinc(pos / np.float32(FRAME) - np.float32(TAPS / 2.0)).astype(np.float32) * (
        np.float32(0.5) - np.float32(0.5) * np.cos(np.float32(2.0 * math.pi) * pos / np.float32(span))
    )
    phase = np.arange(FRAME)[:, None] * np.arange(CH)[None, :] % FRAME
    angle = phase.astype(np.float32) * np.float32(2.0 * math.pi / FRAME)
    basis = np.concatenate([np.cos(angle), -np.sin(angle)], axis=1).astype(np.float32)
    table = window.astype(np.float32).reshape(TAPS, FRAME)[:, :, None] * basis[None]
    table = table * np.float32(2.0 / math.sqrt(FRAME))
    part, core, chip = np.meshgrid(np.arange(4), np.arange(2), np.arange(64), indexing="ij")
    column = (part % 2) * CH + 2 * (2 * chip + core) + part // 2
    return np.ascontiguousarray(table[:, :, column.reshape(-1)].transpose(0, 2, 1)).astype(BF16)


def swap_step(pair, bit, lane):
    low, high = pair
    clear = (lane & bit) == 0
    return (
        jnp.where(clear, low, pltpu.roll(high, bit, 1)),
        jnp.where(clear, pltpu.roll(low, 128 - bit, 1), high),
    )


def kernel(
    samples, history, table, cells_hbm, weights_hbm, out,
    tab, smp, halo, even, odd, spec, turn, hold, mid, relay, full, perm, rhs, lhs, wsm, cells, weights,
    tab_sem, smp_sem, cell_sem, halo_send, halo_recv, own_sem, p1_send, p1_recv, p2_send, p2_recv, a_send, a_recv,
    b_send, b_recv,
):
    ct = lax.axis_index("ct")
    bl = lax.axis_index("bl")
    y = ct // 16
    z = lax.rem(ct // 2, RING)
    c = lax.rem(ct, 2)

    def on(yy, zz, cc):
        return (yy * 16 + zz * 2 + cc, bl)

    barrier = pltpu.get_barrier_semaphore()

    def greet(device):
        pl.semaphore_signal(barrier, inc=1, device_id=device, device_id_type=MESH)

    for k in (1, NX - 1):
        greet((ct, lax.rem(bl + k, NX)))
        greet(on(y, z, 1 - c)[:1] + (lax.rem(bl + k, NX),))
    greet(on(y, z, 1 - c))
    for k in range(1, RING):
        greet(on(lax.rem(y + k, RING), z, c))
        greet(on(y, lax.rem(z + k, RING), c))

    smp_copy = pltpu.make_async_copy(samples, smp, smp_sem)
    smp_copy.start()
    cell_copies = [
        pltpu.make_async_copy(cells_hbm, cells, cell_sem.at[0]),
        pltpu.make_async_copy(weights_hbm, weights, cell_sem.at[1]),
    ]
    for copy in cell_copies:
        copy.start()
    tab_copies = []
    for t in range(TAPS):
        tab_copies.append(pltpu.make_async_copy(table.at[t], tab.at[t], tab_sem.at[t]))
        tab_copies[-1].start()

    pl.semaphore_wait(barrier, 5 + 2 * (RING - 1))

    halo_copy = pltpu.make_async_remote_copy(
        src_ref=samples.at[:, pl.ds((SPEC_DEV - HALO) * FRAME, HALO * FRAME)],
        dst_ref=halo,
        send_sem=halo_send,
        recv_sem=halo_recv,
        device_id=(ct, lax.rem(bl + 1, NX)),
        device_id_type=MESH,
    )
    hist_copy = pltpu.make_async_copy(history, halo, own_sem.at[4])

    @pl.when(bl < NX - 1)
    def _():
        halo_copy.start()

    @pl.when(bl == 0)
    def _():
        hist_copy.start()

    def put(ext, value):
        even[pl.ds(8 * ext, 8), :] = value
        if ext >= 1:
            odd[pl.ds(8 * (ext - 1), 8), :] = value

    smp_copy.wait()
    for f in range(SPEC_DEV):
        put(f + HALO, smp[:, pl.ds(f * FRAME, FRAME)])

    @pl.when(bl < NX - 1)
    def _():
        halo_copy.wait_send()

    @pl.when(bl == 0)
    def _():
        hist_copy.wait()

    @pl.when(bl > 0)
    def _():
        halo_copy.wait_recv()

    for f in range(HALO):
        put(f, halo[:, pl.ds(f * FRAME, FRAME)])

    total = None
    for t in range(TAPS):
        tab_copies[t].wait()
        source = (even, odd)[t % 2]
        term = lax.dot_general(
            tab[t], source[pl.ds(16 * (t // 2), 256), :], (((1,), (1,)), ((), ())), preferred_element_type=F32
        )
        total = term if total is None else total + term
    spec[...] = total

    lane = lax.broadcasted_iota(jnp.int32, (8, 128), 1)
    for g in range(16):
        v = [spec[pl.ds(q * 128 + g * 8, 8), pl.ds(h * 128, 128)] for q in range(4) for h in range(2)]
        for bit in (1, 2, 4):
            for i in range(8):
                if not i & bit:
                    v[i], v[i | bit] = swap_step((v[i], v[i | bit]), bit, lane)
        for p in range(ROWS):
            turn[pl.ds(g * 64 + p, 8, stride=8), :] = v[p]
        hold[g // 8, g % 8] = turn[pl.ds(g * 64, 64), :].astype(BF16).reshape(8, 8, 128)

    def column(k):
        return lax.rem(y + RING - k, RING)

    def depth(k):
        return lax.rem(z + RING - k, RING)

    first = {}
    for n, k in enumerate(OFFSETS):
        far_y, far_z = lax.rem(y + k, RING), lax.rem(z + k, RING)
        first[0, n] = pltpu.make_async_remote_copy(
            src_ref=hold.at[c, :, far_z], dst_ref=mid.at[0, :, z],
            send_sem=p1_send.at[0, n], recv_sem=p1_recv.at[0, n], device_id=on(y, far_z, c), device_id_type=MESH,
        )
        first[1, n] = pltpu.make_async_remote_copy(
            src_ref=hold.at[1 - c, far_y], dst_ref=mid.at[1, y],
            send_sem=p1_send.at[1, n], recv_sem=p1_recv.at[1, n], device_id=on(far_y, z, c), device_id_type=MESH,
        )
        first[0, n].start()
        first[1, n].start()
    keep = [
        pltpu.make_async_copy(hold.at[c, :, z], mid.at[0, :, z], own_sem.at[0]),
        pltpu.make_async_copy(hold.at[1 - c, y], mid.at[1, y], own_sem.at[1]),
        pltpu.make_async_copy(mid.at[0, y], full.at[bl, c, y], own_sem.at[2]),
    ]
    keep[0].start()
    keep[1].start()

    for copy in cell_copies:
        copy.wait()

    def one_weight(t, carry):
        for ch in range(2):
            scaled = weights[ch, t] * (1.0 / math.sqrt(SPECTRA))
            for e in range(CELL_DEV):
                wsm[ch, e, t] = jnp.where(cells[ch, t] == bl * CELL_DEV + e, scaled, 0.0)
        return carry

    lax.fori_loop(0, NTILE, one_weight, 0)

    source = lax.broadcasted_iota(jnp.int32, (256, 512), 0)
    column_id = lax.broadcasted_iota(jnp.int32, (256, 512), 1)
    turned, channel = column_id // 256, (column_id // 128) % 2
    lane_id = (column_id % 128) ^ (2 * turned)
    wanted = ((lane_id // 4) % 2) * 128 + (lane_id & 123) + 4 * channel
    sign = 1 - 2 * turned * (lane_id // 2 % 2)
    perm[...] = jnp.where(source == wanted, sign, 0).astype(F32).astype(BF16)

    right, left = lax.rem(bl + 1, NX), lax.rem(bl + NX - 1, NX)
    sent = list(first.values())

    def push(source, target, send, recv, device):
        copy = pltpu.make_async_remote_copy(
            src_ref=source, dst_ref=target, send_sem=send, recv_sem=recv, device_id=device, device_id_type=MESH
        )
        copy.start()
        sent.append(copy)
        return copy

    def wait_for(sem):
        pltpu.make_async_remote_copy(
            src_ref=relay.at[0], dst_ref=relay.at[0], send_sem=own_sem.at[3], recv_sem=sem,
            device_id=(ct, right), device_id_type=MESH,
        ).wait_recv()

    def share_own(n, k, source):
        target = full.at[bl, c, column(k)]
        source = target if source is None else source
        push(source, target, a_send.at[0, n], a_recv.at[0, n], (ct, right))
        push(source, target, a_send.at[1, n], a_recv.at[1, n], (ct, left))

    def share_other(n, k, source):
        target = full.at[bl, c, :, depth(k)]
        source = relay.at[:, depth(k)] if source is None else source
        push(source, target, b_send.at[0, n], b_recv.at[0, n], on(y, z, 1 - c)[:1] + (right,))
        push(source, target, b_send.at[1, n], b_recv.at[1, n], on(y, z, 1 - c)[:1] + (left,))
        push(source, target, b_send.at[2, n], b_recv.at[2, n], on(y, z, 1 - c))

    def pass_own(n, k):
        wait_for(a_recv.at[0, n])
        chunk = full.at[left, c, column(k)]
        push(chunk, chunk, a_send.at[2, n], a_recv.at[2, n], (ct, right))

    def pass_other(n):
        chunk = full.at[right, 1 - c, :, depth(offset(n))]
        return pltpu.make_async_remote_copy(
            src_ref=chunk, dst_ref=chunk, send_sem=b_send.at[3, n], recv_sem=b_recv.at[3, n],
            device_id=(ct, left), device_id_type=MESH,
        )

    second = {}
    for h in range(2):
        for n in range(RING - 1):
            first[h, n].wait_recv()
        keep[h].wait()
        for n, k in enumerate(OFFSETS):
            far_y, far_z = lax.rem(y + k, RING), lax.rem(z + k, RING)
            if h == 0:
                second[h, n] = push(
                    mid.at[0, far_y], full.at[bl, c, y], p2_send.at[0, n], p2_recv.at[0, n], on(far_y, z, c)
                )
            else:
                second[h, n] = push(
                    mid.at[1, :, far_z], relay.at[:, z], p2_send.at[1, n], p2_recv.at[1, n], on(y, far_z, c)
                )
        if h == 0:
            share_own(0, 0, mid.at[0, y])
            keep[2].start()
        else:
            share_other(0, 0, mid.at[1, :, z])
    for n, k in enumerate(OFFSETS):
        second[0, n].wait_recv()
        share_own(n + 1, k, None)
    for n, k in enumerate(OFFSETS):
        second[1, n].wait_recv()
        share_other(n + 1, k, None)
    for n, k in enumerate((0,) + OFFSETS):
        pass_own(n, k)
    for n in range(RING):
        wait_for(b_recv.at[1, n])
        pass_other(n).start()
    keep[2].wait()
    for n in range(RING):
        wait_for(a_recv.at[1, n])
        wait_for(b_recv.at[0, n])
        wait_for(b_recv.at[2, n])

    def operands(pair, time, j):
        d = [
            jnp.concatenate([full[2 * time + b, :, jj, zz].reshape(16, 128) for jj in (j, j + 1) for zz in range(RING)], axis=0)
            for b in range(2)
        ]
        moved = jnp.dot(jnp.concatenate(d, axis=1), perm[...], preferred_element_type=F32).astype(BF16)
        for jj in range(2):
            for ch in range(2):
                for part in range(2):
                    rhs[pair, ch, part * 128:(part + 1) * 128, (j + jj) * 128:(j + jj + 1) * 128] = moved[
                        jj * 128:(jj + 1) * 128, part * 256 + ch * 128:part * 256 + (ch + 1) * 128
                    ]

    def fold(pair, zz):
        rows = pl.ds(pl.multiple_of(zz * 16, 16), 16)
        for ch in range(2):
            x = [rhs[pair, ch, rows, i * 128:(i + 1) * 128].astype(F32) for i in range(8)]
            for e in range(CELL_DEV):
                place = pl.ds(pl.multiple_of(e * 128 + zz * 16, 16), 16)
                for j in range(8):
                    acc = None
                    for i in range(j + 1):
                        t = i * 8 - i * (i - 1) // 2 + j - i
                        term = x[i] * wsm[ch, e, t]
                        acc = term if acc is None else acc + term
                    lhs[pair, ch, place, j * 128:(j + 1) * 128] = acc.astype(BF16)

    def products(pair, time):
        def slab(zz, carry):
            fold(pair, zz)
            return carry

        for j in range(0, 8, 2):
            operands(pair, time, j)
        lax.fori_loop(0, RING, slab, 0)
        for ch in range(2):
            result = lax.dot_general(
                lhs[pair, ch], rhs[pair, ch], (((1,), (1,)), ((), ())), preferred_element_type=F32
            )
            for e in range(CELL_DEV):
                for x in range(2):
                    value = result[e * 128:(e + 1) * 128, x * 128:(x + 1) * 128]
                    out[e, ch, x] = value if pair == 0 else out[e, ch, x] + value

    products(0, bl // 2)
    for n in range(RING):
        wait_for(a_recv.at[2, n])
        wait_for(b_recv.at[3, n])
    products(1, 1 - bl // 2)

    for copy in sent:
        copy.wait_send()
    for n in range(RING):
        pass_other(n).wait_send()


def shards(samples, history, tile_cell, tile_weight):
    table = jnp.asarray(filter_table())
    hbm = pl.BlockSpec(memory_space=pltpu.HBM)
    dma = pltpu.SemaphoreType.DMA
    return pl.pallas_call(
        kernel,
        out_shape=jax.ShapeDtypeStruct((CELL_DEV, 2, 2, BLOCK, BLOCK), F32),
        in_specs=[hbm] * 5,
        out_specs=pl.BlockSpec(memory_space=pltpu.VMEM),
        scratch_shapes=[
            pltpu.VMEM((TAPS, 2 * CH, FRAME), BF16),
            pltpu.VMEM((8, SPEC_DEV * FRAME), BF16),
            pltpu.VMEM((8, HALO * FRAME), BF16),
            pltpu.VMEM((288, FRAME), BF16),
            pltpu.VMEM((288, FRAME), BF16),
            pltpu.VMEM((512, 256), F32),
            pltpu.VMEM((1024, 128), F32),
            pltpu.VMEM((2, RING, RING, 8, 128), BF16),
            pltpu.VMEM((2, RING, RING, 8, 128), BF16),
            pltpu.VMEM((RING, RING, 8, 128), BF16),
            pltpu.VMEM((NX, 2, RING, RING, 8, 128), BF16),
            pltpu.VMEM((256, 512), BF16),
            pltpu.VMEM((2, 2, 256, 1024), BF16),
            pltpu.VMEM((2, 2, 256, 1024), BF16),
            pltpu.SMEM((2, CELL_DEV, NTILE), F32),
            pltpu.SMEM((2, NTILE), jnp.int32),
            pltpu.SMEM((2, NTILE), F32),
            dma((TAPS,)),
            dma,
            dma((2,)),
            dma,
            dma,
            dma((5,)),
            dma((2, RING - 1)),
            dma((2, RING - 1)),
            dma((2, RING - 1)),
            dma((2, RING - 1)),
            dma((3, RING)),
            dma((3, RING)),
            dma((4, RING)),
            dma((4, RING)),
        ],
        compiler_params=pltpu.CompilerParams(
            collective_id=0, has_side_effects=True, vmem_limit_bytes=40 * 1024 * 1024
        ),
    )(*[pltpu.with_memory_space_constraint(v, pltpu.HBM) for v in (samples, history, table, tile_cell, tile_weight)])


def solution(mesh):
    return jax.shard_map(
        shards,
        mesh=mesh,
        in_specs=(P("ct", "bl"), P("ct", None), P("ct", None), P("ct", None)),
        out_specs=P("bl", "ct", None, None, None),
        check_vma=False,
    )
```

time: 44 us -> 42.5 us (0.966)
  the two profiles are of different devices: /device:TPU:8 before, /device:TPU:1 now
where the time goes in v3:
time: 42.5 us; the launch traced here: 42.3 us
  Pallas kernels  41.5 us (98%)
  local copies, waits for them, and re-layouts  0.8 us (2%)
    pallas_call x1, Pallas kernels, shards(): pl.pallas_call(kernel, out_shape=jax.ShapeDtypeStruct((CELL_DEV, 2, 2, BL...  41.5 us

profile of v3, /device:TPU:1, one launch (start us, length us, event | category | flops | bytes accessed | tf_op | source)
XLA Modules:
  0.0 42.3 jit_solution(14002325080611831429)
XLA Ops:
  0.0 41.5 %shard_map.55 = f32[2,2,2,128,128]{4,3,2,1,0:T(8,128)S(1)} custom-call(bf16[8,16384]{1,0:T(8,128)(2,1)} %samples.1, bf16[8,1536]{1,0:T(8,128)(2,1)} %history.1, bf16[4,512,512]{2,1,0:T(8,128)(2,1)} %constant.2.clone.table, s32[2,36]{1,0:T(2,128)} %cells_hbm.1, f32[2,36]{1,0:T(2,128)} %weights_hbm.1), custom_call_target="tpu_custom_call" | custom-call | tf_op jit(solution)/shard_map/pallas_call | solution.py:356
  41.6 0.8 %copy.7 = f32[2,2,2,128,128]{4,3,2,1,0:T(8,128)} copy(f32[2,2,2,128,128]{4,3,2,1,0:T(8,128)S(1)} %shard_map.55) | data formatting | bytes 1048576

commit v4 on v3

--- a/solution.py
+++ b/solution.py
@@ -34,6 +34,7 @@
 
 
 OFFSETS = tuple(offset(n) for n in range(1, RING))
+NEAREST = tuple(reversed(tuple(enumerate(OFFSETS))))
 
 
 def filter_table():
@@ -49,7 +50,8 @@
     table = table * np.float32(2.0 / math.sqrt(FRAME))
     part, core, chip = np.meshgrid(np.arange(4), np.arange(2), np.arange(64), indexing="ij")
     column = (part % 2) * CH + 2 * (2 * chip + core) + part // 2
-    return np.ascontiguousarray(table[:, :, column.reshape(-1)].transpose(0, 2, 1)).astype(BF16)
+    rows = table[:, :, column.reshape(-1)].transpose(2, 0, 1).reshape(2 * CH, span)
+    return np.ascontiguousarray(rows).astype(BF16)
 
 
 def swap_step(pair, bit, lane):
@@ -63,7 +65,7 @@
 
 def kernel(
     samples, history, table, cells_hbm, weights_hbm, out,
-    tab, smp, halo, even, odd, spec, turn, hold, mid, relay, full, perm, rhs, lhs, wsm, cells, weights,
+    tab, smp, halo, taps, spec, turn, hold, mid, relay, full, perm, rhs, lhs, wsm, cells, weights,
     tab_sem, smp_sem, cell_sem, halo_send, halo_recv, own_sem, p1_send, p1_recv, p2_send, p2_recv, a_send, a_recv,
     b_send, b_recv,
 ):
@@ -97,10 +99,8 @@
     ]
     for copy in cell_copies:
         copy.start()
-    tab_copies = []
-    for t in range(TAPS):
-        tab_copies.append(pltpu.make_async_copy(table.at[t], tab.at[t], tab_sem.at[t]))
-        tab_copies[-1].start()
+    tab_copy = pltpu.make_async_copy(table, tab, tab_sem)
+    tab_copy.start()
 
     pl.semaphore_wait(barrier, 5 + 2 * (RING - 1))
 
@@ -123,9 +123,9 @@
         hist_copy.start()
 
     def put(ext, value):
-        even[pl.ds(8 * ext, 8), :] = value
-        if ext >= 1:
-            odd[pl.ds(8 * (ext - 1), 8), :] = value
+        for t in range(TAPS):
+            if 0 <= ext - t < SPEC_DEV:
+                taps[pl.ds(8 * (ext - t), 8), t * FRAME:(t + 1) * FRAME] = value
 
     smp_copy.wait()
     for f in range(SPEC_DEV):
@@ -146,49 +146,54 @@
     for f in range(HALO):
         put(f, halo[:, pl.ds(f * FRAME, FRAME)])
 
-    total = None
-    for t in range(TAPS):
-        tab_copies[t].wait()
-        source = (even, odd)[t % 2]
-        term = lax.dot_general(
-            tab[t], source[pl.ds(16 * (t // 2), 256), :], (((1,), (1,)), ((), ())), preferred_element_type=F32
-        )
-        total = term if total is None else total + term
-    spec[...] = total
+    tab_copy.wait()
+    spec[...] = lax.dot_general(tab[...], taps[...], (((1,), (1,)), ((), ())), preferred_element_type=F32)
 
     lane = lax.broadcasted_iota(jnp.int32, (8, 128), 1)
-    for g in range(16):
-        v = [spec[pl.ds(q * 128 + g * 8, 8), pl.ds(h * 128, 128)] for q in range(4) for h in range(2)]
+    def column(k):
+        return lax.rem(y + RING - k, RING)
+
+    def depth(k):
+        return lax.rem(z + RING - k, RING)
+
+    def to_rows(core, which, chips):
+        at = core * 64 + chips * 8
+        v = [
+            spec[pl.ds(pl.multiple_of(q * 128 + at, 8), 8), pl.ds(h * 128, 128)]
+            for q in range(4)
+            for h in range(2)
+        ]
         for bit in (1, 2, 4):
             for i in range(8):
                 if not i & bit:
                     v[i], v[i | bit] = swap_step((v[i], v[i | bit]), bit, lane)
+        place = which * 512 + chips * 64
         for p in range(ROWS):
-            turn[pl.ds(g * 64 + p, 8, stride=8), :] = v[p]
-        hold[g // 8, g % 8] = turn[pl.ds(g * 64, 64), :].astype(BF16).reshape(8, 8, 128)
-
-    def column(k):
-        return lax.rem(y + RING - k, RING)
-
-    def depth(k):
-        return lax.rem(z + RING - k, RING)
+            turn[pl.ds(place + p, 8, stride=8), :] = v[p]
+        hold[which, chips] = turn[pl.ds(place, 64), :].astype(BF16).reshape(8, 8, 128)
 
     first = {}
+    for chips in range(8):
+        to_rows(c, 0, chips)
     for n, k in enumerate(OFFSETS):
-        far_y, far_z = lax.rem(y + k, RING), lax.rem(z + k, RING)
+        far_z = lax.rem(z + k, RING)
         first[0, n] = pltpu.make_async_remote_copy(
-            src_ref=hold.at[c, :, far_z], dst_ref=mid.at[0, :, z],
+            src_ref=hold.at[0, :, far_z], dst_ref=mid.at[0, :, z],
             send_sem=p1_send.at[0, n], recv_sem=p1_recv.at[0, n], device_id=on(y, far_z, c), device_id_type=MESH,
         )
+        first[0, n].start()
+    for chips in range(8):
+        to_rows(1 - c, 1, chips)
+    for n, k in enumerate(OFFSETS):
+        far_y = lax.rem(y + k, RING)
         first[1, n] = pltpu.make_async_remote_copy(
-            src_ref=hold.at[1 - c, far_y], dst_ref=mid.at[1, y],
+            src_ref=hold.at[1, far_y], dst_ref=mid.at[1, y],
             send_sem=p1_send.at[1, n], recv_sem=p1_recv.at[1, n], device_id=on(far_y, z, c), device_id_type=MESH,
         )
-        first[0, n].start()
         first[1, n].start()
     keep = [
-        pltpu.make_async_copy(hold.at[c, :, z], mid.at[0, :, z], own_sem.at[0]),
-        pltpu.make_async_copy(hold.at[1 - c, y], mid.at[1, y], own_sem.at[1]),
+        pltpu.make_async_copy(hold.at[0, :, z], mid.at[0, :, z], own_sem.at[0]),
+        pltpu.make_async_copy(hold.at[1, y], mid.at[1, y], own_sem.at[1]),
         pltpu.make_async_copy(mid.at[0, y], full.at[bl, c, y], own_sem.at[2]),
     ]
     keep[0].start()
@@ -276,15 +281,16 @@
             keep[2].start()
         else:
             share_other(0, 0, mid.at[1, :, z])
-    for n, k in enumerate(OFFSETS):
+    for n, k in NEAREST:
         second[0, n].wait_recv()
         share_own(n + 1, k, None)
-    for n, k in enumerate(OFFSETS):
+    for n, k in NEAREST:
         second[1, n].wait_recv()
         share_other(n + 1, k, None)
-    for n, k in enumerate((0,) + OFFSETS):
-        pass_own(n, k)
-    for n in range(RING):
+    pass_own(0, 0)
+    for n, k in NEAREST:
+        pass_own(n + 1, k)
+    for n in (0,) + tuple(n + 1 for n, k in NEAREST):
         wait_for(b_recv.at[1, n])
         pass_other(n).start()
     keep[2].wait()
@@ -359,11 +365,10 @@
         in_specs=[hbm] * 5,
         out_specs=pl.BlockSpec(memory_space=pltpu.VMEM),
         scratch_shapes=[
-            pltpu.VMEM((TAPS, 2 * CH, FRAME), BF16),
+            pltpu.VMEM((2 * CH, TAPS * FRAME), BF16),
             pltpu.VMEM((8, SPEC_DEV * FRAME), BF16),
             pltpu.VMEM((8, HALO * FRAME), BF16),
-            pltpu.VMEM((288, FRAME), BF16),
-            pltpu.VMEM((288, FRAME), BF16),
+            pltpu.VMEM((8 * SPEC_DEV, TAPS * FRAME), BF16),
             pltpu.VMEM((512, 256), F32),
             pltpu.VMEM((1024, 128), F32),
             pltpu.VMEM((2, RING, RING, 8, 128), BF16),
@@ -376,7 +381,7 @@
             pltpu.SMEM((2, CELL_DEV, NTILE), F32),
             pltpu.SMEM((2, NTILE), jnp.int32),
             pltpu.SMEM((2, NTILE), F32),
-            dma((TAPS,)),
+            dma,
             dma,
             dma((2,)),
             dma,

time: 42.5 us -> 41.6 us (0.979)
  Pallas kernels: 41.5 us -> 40.7 us
    pallas_call x1, Pallas kernels: 41.5 us -> 40.7 us  [shards(): pl.pallas_call(kernel, out_shape=jax.ShapeDtypeStruct((CELL_DEV, 2, 2, BL...]
where the time goes in v4:
time: 41.6 us; the launch traced here: 41.5 us
  Pallas kernels  40.7 us (98%)
  local copies, waits for them, and re-layouts  0.8 us (2%)
    pallas_call x1, Pallas kernels, shards(): pl.pallas_call(kernel, out_shape=jax.ShapeDtypeStruct((CELL_DEV, 2, 2, BL...  40.7 us

profile of v4, /device:TPU:1, one launch (start us, length us, event | category | flops | bytes accessed | tf_op | source)
XLA Modules:
  0.0 41.5 jit_solution(14032036861785433746)
XLA Ops:
  0.0 40.7 %shard_map.55 = f32[2,2,2,128,128]{4,3,2,1,0:T(8,128)S(1)} custom-call(bf16[8,16384]{1,0:T(8,128)(2,1)} %samples.1, bf16[8,1536]{1,0:T(8,128)(2,1)} %history.1, bf16[512,2048]{1,0:T(8,128)(2,1)} %constant.2.clone.table, s32[2,36]{1,0:T(2,128)} %cells_hbm.1, f32[2,36]{1,0:T(2,128)} %weights_hbm.1), custom_call_target="tpu_custom_call" | custom-call | tf_op jit(solution)/shard_map/pallas_call | solution.py:362
  40.7 0.8 %copy.7 = f32[2,2,2,128,128]{4,3,2,1,0:T(8,128)} copy(f32[2,2,2,128,128]{4,3,2,1,0:T(8,128)S(1)} %shard_map.55) | data formatting | bytes 1048576

commit v5 on v4

--- a/solution.py
+++ b/solution.py
@@ -287,12 +287,14 @@
     for n, k in NEAREST:
         second[1, n].wait_recv()
         share_other(n + 1, k, None)
-    pass_own(0, 0)
-    for n, k in NEAREST:
-        pass_own(n + 1, k)
-    for n in (0,) + tuple(n + 1 for n, k in NEAREST):
-        wait_for(b_recv.at[1, n])
-        pass_other(n).start()
+    order = ((-1, 0),) + NEAREST
+    for i in range(RING + 3):
+        if i < RING:
+            pass_own(order[i][0] + 1, order[i][1])
+        if i >= 3:
+            n = order[i - 3][0] + 1
+            wait_for(b_recv.at[1, n])
+            pass_other(n).start()
     keep[2].wait()
     for n in range(RING):
         wait_for(a_recv.at[1, n])

time: 41.6 us -> 41.5 us (level)
  no operation moved by 1% of the time
where the time goes in v5:
time: 41.5 us; the launch traced here: 41.4 us
  Pallas kernels  40.5 us (98%)
  local copies, waits for them, and re-layouts  0.8 us (2%)
    pallas_call x1, Pallas kernels, shards(): pl.pallas_call(kernel, out_shape=jax.ShapeDtypeStruct((CELL_DEV, 2, 2, BL...  40.5 us

profile of v5, /device:TPU:1, one launch (start us, length us, event | category | flops | bytes accessed | tf_op | source)
XLA Modules:
  0.0 41.4 jit_solution(13199204254542854701)
XLA Ops:
  0.0 40.5 %shard_map.55 = f32[2,2,2,128,128]{4,3,2,1,0:T(8,128)S(1)} custom-call(bf16[8,16384]{1,0:T(8,128)(2,1)} %samples.1, bf16[8,1536]{1,0:T(8,128)(2,1)} %history.1, bf16[512,2048]{1,0:T(8,128)(2,1)} %constant.2.clone.table, s32[2,36]{1,0:T(2,128)} %cells_hbm.1, f32[2,36]{1,0:T(2,128)} %weights_hbm.1), custom_call_target="tpu_custom_call" | custom-call | tf_op jit(solution)/shard_map/pallas_call | solution.py:364
  40.6 0.8 %copy.7 = f32[2,2,2,128,128]{4,3,2,1,0:T(8,128)} copy(f32[2,2,2,128,128]{4,3,2,1,0:T(8,128)S(1)} %shard_map.55) | data formatting | bytes 1048576
